TPU v7x, 32 devices: a whole 2x2x4 slice. The times are simulated.
32 devices in a mesh: prow: 4 (over x, core), pcol: 8 (over z, y).
Axes of the slice: x: 2, y: 2, z: 4, core: 2. Of those that a mesh axis runs over, the one named last changes fastest.
Arguments:
- inverse_blocks: bfloat16 [7168, 7168], P('prow', 'pcol'), may hold values from -6 to 6
- lower_late: bfloat16 [56, 128, 256], P('prow', 'pcol'), may hold values from -0.09375 to 0.09375
- lower_early: bfloat16 [56, 128, 256], P('prow', 'pcol'), may hold values from -0.09375 to 0.09375
- link_block: bfloat16 [256, 256], replicated, may hold values from -0.375 to 0.375
- diag_inverse: float32 [2, 256, 256], replicated, may hold values from -6 to 6
- structures: int32 [2, 28], replicated, may hold values from 0 to 55, as said below
Outputs:
- panel_late: float32 [56, 128, 256], P('prow', 'pcol')
- diag_late: float32 [256, 256], replicated
- panel_early: float32 [56, 128, 256], P('prow', 'pcol')
- cross_block: float32 [256, 256], replicated
- diag_early: float32 [256, 256], replicated
Inputs may be any that keep to these rules, and one draw needn't show every extreme that they name: `structures`: each row lists 28 different block numbers in increasing order. Among the 14 blocks with the same value of n // 14 at most 10 are listed, and in each row some such group has exactly 10.
All inputs are finite; a program needn't handle non-finite values.
Results may differ from a plain program's by a relative error of at most 0.01.
Values may be sent and summed in bfloat16 or wider, within the bound.
A program may use at most 64 MiB of HBM per device.

v0:
```python
import jax
import jax.numpy as jnp
from jax import lax
from jax.sharding import PartitionSpec as P

WIDTH = 256
BLK = 128


def from_root(value, axis, source):
    kept = jnp.where(lax.axis_index(axis) == source, value, 0).astype(value.dtype)
    return lax.psum(kept, axis)


def split_parts(values):
    upper = values.astype(jnp.bfloat16)
    lower = (values - upper.astype(jnp.float32)).astype(jnp.bfloat16)
    return (upper, lower)


def rows_product(left, right_float):
    upper, lower = split_parts(right_float)
    dims = (((0,), (0,)), ((), ()))
    first = lax.dot_general(left, upper, dims, preferred_element_type=jnp.float32)
    return first + lax.dot_general(left, lower, dims, preferred_element_type=jnp.float32)


def shards(inverse_blocks, lower_late, lower_early, link_block, diag_inverse, structures):
    high = lax.Precision.HIGHEST
    row_blocks = inverse_blocks.shape[0] // BLK
    col_blocks = inverse_blocks.shape[1] // BLK
    row_id = lax.axis_index("prow")
    col_id = lax.axis_index("pcol")
    block_ids = row_id * row_blocks + jnp.arange(row_blocks, dtype=jnp.int32)

    def block_hits(listed):
        return jnp.any(listed[:, None] == block_ids[None, :], axis=0).astype(jnp.float32)

    def own_columns(strip):
        return lax.dynamic_slice_in_dim(strip, col_id % 2 * col_blocks, col_blocks, 0)

    def reduce_columns(columns, flag_list):
        count = len(flag_list)
        product = jnp.dot(inverse_blocks, columns, preferred_element_type=jnp.float32)
        summed = lax.psum_scatter(
            product.reshape(row_blocks, BLK, count * WIDTH).astype(jnp.bfloat16),
            "pcol",
            scatter_dimension=1,
            tiled=True,
        ).astype(jnp.float32)
        return [summed]

    def separate_reduce(masked, hit_flags):
        strip = lax.all_gather(masked, "pcol", axis=1, tiled=True)
        columns = from_root(own_columns(strip), "prow", col_id // 2)
        columns = columns.reshape(col_blocks * BLK, WIDTH)
        return reduce_columns(columns, [hit_flags])[0]

    hits_late = block_hits(structures[0])
    hits_early = block_hits(structures[1])
    masked_late = lower_late * hits_late.astype(jnp.bfloat16)[:, None, None]
    masked_early = lower_early * hits_early.astype(jnp.bfloat16)[:, None, None]
    late_rows = masked_late.reshape(-1, WIDTH)
    early_rows = masked_early.reshape(-1, WIDTH)
    link_float = link_block.astype(jnp.float32)
    reduced_late = separate_reduce(masked_late, hits_late)
    reduced_early = separate_reduce(masked_early, hits_early)
    panel_late = -(reduced_late * hits_late[:, None, None])
    late_flat = panel_late.reshape(-1, WIDTH)
    local_late = rows_product(late_rows, late_flat)
    cross_local = rows_product(early_rows, late_flat).T
    sum_late = lax.psum(local_late, ("prow", "pcol"))
    diag_late = diag_inverse[0] - sum_late
    flat_upper, flat_lower = split_parts(late_flat)
    carried = jnp.dot(flat_upper, link_block, preferred_element_type=jnp.float32) + jnp.dot(
        flat_lower, link_block, preferred_element_type=jnp.float32
    )
    panel_early = -(
        (reduced_early + carried.reshape(reduced_early.shape)) * hits_early[:, None, None]
    )
    local_early = rows_product(early_rows, panel_early.reshape(-1, WIDTH))
    sum_early, cross_sum = lax.psum((local_early, cross_local), ("prow", "pcol"))
    cross_block = -cross_sum - jnp.dot(diag_late, link_float, precision=high)
    diag_early = diag_inverse[1] - sum_early - jnp.dot(link_float.T, cross_block, precision=high)
    return (panel_late, diag_late, panel_early, cross_block, diag_early)


def solution(mesh):
    placed = (P("prow", "pcol"), P("prow", "pcol", None), P("prow", "pcol", None), P(), P(), P())
    return jax.shard_map(
        shards,
        mesh=mesh,
        in_specs=placed,
        out_specs=(P("prow", "pcol", None), P(), P("prow", "pcol", None), P(), P()),
        check_vma=False,
    )
```

profile of v0, /device:TPU:0, one launch (start us, length us, event | category | flops | bytes accessed | tf_op | source)
XLA Modules:
  0.0 405.6 jit_solution(15092679226556821970)
XLA Ops:
  8.3 1.0 broadcast_multiply_fusion
  9.3 36.2 %all_gather.7 = bf16[14,128,256]{2,1,0:T(8,128)(2,1)} all-gather(bf16[14,16,256]{2,1,0:T(8,128)(2,1)S(1)} %broadcast_multiply_fusion), channel_id=1, replica_groups=mesh['prow'=4,'pcol'=8] {'pcol'}, dimensions={1}, use_global_device_ids=true | all-gather | bytes 1032192 | tf_op jit(solution)/shard_map/all_gather | solution.py:54
  45.5 1.0 broadcast_multiply_fusion.1
  47.1 34.3 %all_gather.6 = bf16[14,128,256]{2,1,0:T(8,128)(2,1)} all-gather(bf16[14,16,256]{2,1,0:T(8,128)(2,1)S(1)} %broadcast_multiply_fusion.1), channel_id=1, replica_groups=mesh['prow'=4,'pcol'=8] {'pcol'}, dimensions={1}, use_global_device_ids=true | all-gather | bytes 1032192 | tf_op jit(solution)/shard_map/all_gather | solution.py:54
  81.5 1.8 dynamic-slice_select_fusion
  83.3 1.8 dynamic-slice_select_fusion.1
  85.2 37.1 %all-reduce.7.cloned.1.call-done = (bf16[896,256]{1,0:T(8,128)(2,1)}, bf16[896,256]{1,0:T(8,128)(2,1)}) async-done(((bf16[896,256]{1,0:T(8,128)(2,1)}, bf16[896,256]{1,0:T(8,128)(2,1)}), (bf16[896,256]{1,0:T(8,128)(2,1)}, bf16[896,256]{1,0:T(8,128)(2,1)})) %all-reduce.7.cloned.1.call-update) | async-done | bytes 917520 | tf_op jit(solution)/shard_map/psum | solution.py:12
  122.3 3.2 fusion
  125.5 2.2 copy.17
  127.7 3.1 fusion.1
  130.9 2.3 copy.18
  133.2 59.1 %reduce-scatter.3.cloned.1.call-done = bf16[14,16,256]{2,1,0:T(8,128)(2,1)} async-done(((bf16[14,128,256]{2,1,0:T(8,128)(2,1)}), bf16[14,16,256]{2,1,0:T(8,128)(2,1)}) %reduce-scatter.3.cloned.1.call-update) | async-done | bytes 114704 | tf_op jit(solution)/shard_map/reduce_scatter | solution.py:45
  192.3 1.0 multiply_negate_fusion.1
  193.3 0.9 convolution_bitcast_fusion.3
  194.2 1.8 convolution_bitcast_fusion.5
  197.2 62.1 %reduce-scatter.5.cloned.1.call-done = bf16[14,16,256]{2,1,0:T(8,128)(2,1)} async-done(((bf16[14,128,256]{2,1,0:T(8,128)(2,1)}), bf16[14,16,256]{2,1,0:T(8,128)(2,1)}) %reduce-scatter.5.cloned.1.call-update) | async-done | bytes 114704 | tf_op jit(solution)/shard_map/reduce_scatter | solution.py:45
  259.3 1.2 multiply_negate_fusion
  260.7 0.9 fusion.5
  261.6 0.9 fusion.4
  262.6 0.9 fusion.3
  263.5 130.9 %all-reduce.5.cloned.1.call-done = (f32[256,256]{1,0:T(8,128)}, f32[256,256]{1,0:T(8,128)}, f32[256,256]{1,0:T(8,128)}) async-done(((f32[256,256]{1,0:T(8,128)}, f32[256,256]{1,0:T(8,128)}, f32[256,256]{1,0:T(8,128)}), (f32[256,256]{1,0:T(8,128)}, f32[256,256]{1,0:T(8,128)}, f32[256,256]{1,0:T(8,128)})) %all-reduce.5.cloned.1.call-update) | async-done | bytes 786448 | tf_op jit(solution)/shard_map/psum | solution.py:72
  394.5 1.1 bitcast_subtract_fusion.1
  395.6 1.3 convolution_subtract_fusion
  396.9 2.1 fusion.2
  (38 shorter events, 3.3 us)
Async XLA Ops:
  7.2 115.1 %copy-start = (bf16[1792,896]{1,0:T(8,128)(2,1)S(1)}, bf16[1792,896]{1,0:T(8,128)(2,1)}, u32[]{:S(2)}) copy-start(bf16[1792,896]{1,0:T(8,128)(2,1)} %param.6) | copy-start | bytes 9633796
  7.2 115.1 %all-reduce.7.cloned.1.call-start = ((), (), s32[]{:S(2)}) async-start(), calls=%async_computation.5 | async-start | bytes 1835008 | tf_op jit(solution)/shard_map/psum | solution.py:12
  46.5 0.7 copy-start.6
  85.2 107.1 %reduce-scatter.3.cloned.1.call-start = ((), (), s32[]{:S(2)}) async-start(), calls=%async_computation.2 | async-start | bytes 1032192 | tf_op jit(solution)/shard_map/reduce_scatter | solution.py:45
  127.7 131.6 %reduce-scatter.5.cloned.1.call-start = ((), (), s32[]{:S(2)}) async-start(), calls=%async_computation.3 | async-start | bytes 1032192 | tf_op jit(solution)/shard_map/reduce_scatter | solution.py:45
  130.9 65.2 %copy-start.1 = (bf16[256,256]{1,0:T(8,128)(2,1)S(1)}, bf16[256,256]{1,0:T(8,128)(2,1)}, u32[]{:S(2)}) copy-start(bf16[256,256]{1,0:T(8,128)(2,1)} %param.9) | copy-start | bytes 393220
  133.1 261.4 %all-reduce.5.cloned.1.call-start = ((), (), s32[]{:S(2)}) async-start(), calls=%async_computation.4 | async-start | bytes 1572864 | tf_op jit(solution)/shard_map/psum | solution.py:72
  193.3 2.8 copy-start.4
  259.3 2.4 copy-start.5
  259.3 2.4 copy-start.10
  259.3 3.3 copy-start.7
  259.3 3.3 copy-start.9
  260.5 2.1 copy-start.8
  395.6 3.5 copy-start.2
  396.9 2.2 copy-start.3
Sparse Core Ops, SparseCore 0:
  85.3 36.9 all-reduce.6
  127.8 64.4 reduce-scatter.2
  196.0 63.1 reduce-scatter.4
  265.2 129.2 all-reduce.4
where the time goes:
time: 406 us
  waiting for transfers between devices  289 us (71%)
  blocking collectives  70.5 us (17%)
  matrix products  16.6 us (4%)
  between operations  13.9 us (3%)
  other arithmetic  9.06 us (2%)
  local copies, waits for them, and re-layouts  6.03 us (1%)
    psum x1, waiting for transfers between devices, shards(): sum_late = lax.psum(local_late, ('prow', 'pcol'))  131 us
    reduce_scatter x2, waiting for transfers between devices, reduce_columns(): lax.psum_scatter(product.reshape(row_blocks, BLK, count * WIDTH).astype(j...  121 us
    all_gather x2, blocking collectives, separate_reduce(): strip = lax.all_gather(masked, 'pcol', axis=1, tiled=True)  70.5 us
    psum x1, waiting for transfers between devices, from_root(): return lax.psum(kept, axis)  37.1 us
  transfers between devices with their start and end apart: 4, of which 4 were waited for; matrix products, arithmetic and copies ran while one was open for 3% of the time, Pallas kernels for 0%

commit v1 on v0

--- a/solution.py
+++ b/solution.py
@@ -1,6 +1,10 @@
+import functools
+
 import jax
 import jax.numpy as jnp
 from jax import lax
+from jax.experimental import pallas as pl
+from jax.experimental.pallas import tpu as pltpu
 from jax.sharding import PartitionSpec as P
 
 WIDTH = 256
@@ -25,7 +29,7 @@
     return first + lax.dot_general(left, lower, dims, preferred_element_type=jnp.float32)
 
 
-def shards(inverse_blocks, lower_late, lower_early, link_block, diag_inverse, structures):
+def plain_shards(inverse_blocks, lower_late, lower_early, link_block, diag_inverse, structures):
     high = lax.Precision.HIGHEST
     row_blocks = inverse_blocks.shape[0] // BLK
     col_blocks = inverse_blocks.shape[1] // BLK
@@ -85,8 +89,439 @@
     return (panel_late, diag_late, panel_early, cross_block, diag_early)
 
 
+GRID_ROWS = 4
+GRID_COLS = 8
+DEPTH = 4
+MOST = 10
+SPARE = 4
+LANES = 128
+F32 = jnp.float32
+BF16 = jnp.bfloat16
+MESH = pl.DeviceIdType.MESH
+
+
+def fits_kernel(mesh, inverse_blocks, lower_late):
+    sizes = (mesh.shape["prow"], mesh.shape["pcol"])
+    return (
+        sizes == (GRID_ROWS, GRID_COLS)
+        and lower_late.shape == (14, BLK // GRID_COLS, WIDTH)
+        and inverse_blocks.shape == (14 * BLK, 7 * BLK)
+    )
+
+
+def turned(left, right):
+    return lax.dot_general(left, right, (((0,), (0,)), ((), ())), preferred_element_type=F32)
+
+
+def step_kernel(
+    inverse_hbm, late_ref, early_ref, link_ref, diag_ref, structures_ref,
+    panel_late_ref, diag_late_ref, panel_early_ref, cross_ref, diag_early_ref,
+    inverse, masked, columns, wide, product, from_y, to_z, from_z, summed,
+    sums, sums_wide, plane_in, depth_in, totals,
+    inverse_sem, first_send, first_recv, core_send, core_recv, x_send, x_recv,
+    relay_send, relay_recv, y_send, y_recv, z_send, z_recv,
+    plane_send, plane_recv, depth_send, depth_recv, total_send, total_recv,
+):
+    row_id = lax.axis_index("prow")
+    col_id = lax.axis_index("pcol")
+    z_id = col_id // 2
+    y_id = lax.rem(col_id, 2)
+    blocks, rows, _ = late_ref.shape
+    half = blocks // 2
+    listed = structures_ref.shape[1]
+    core_peer = row_id + 1 - 2 * lax.rem(row_id, 2)
+    x_peer = lax.rem(row_id + 2, GRID_ROWS)
+
+    inverse_copy = pltpu.make_async_copy(inverse_hbm, inverse, inverse_sem)
+    inverse_copy.start()
+
+    barrier = pltpu.get_barrier_semaphore()
+    for step in range(1, GRID_ROWS * GRID_COLS):
+        other = lax.rem(row_id * GRID_COLS + col_id + step, GRID_ROWS * GRID_COLS)
+        pl.semaphore_signal(
+            barrier,
+            inc=1,
+            device_id=(other // GRID_COLS, lax.rem(other, GRID_COLS)),
+            device_id_type=MESH,
+        )
+
+    hits, kept, dropped = [], [], []
+    for panel in range(2):
+        lowest = row_id * blocks
+        entries = [structures_ref[panel, entry] - lowest for entry in range(listed)]
+        unlisted = jnp.int32(0)
+        panel_hits, panel_kept, panel_dropped = [], [], []
+        for block in range(blocks):
+            hit = jnp.int32(0)
+            for entry in entries:
+                hit += (entry == block).astype(jnp.int32)
+            drop = (1 - hit) * (unlisted < SPARE).astype(jnp.int32)
+            panel_hits.append(hit.astype(F32))
+            panel_kept.append(1 - drop)
+            panel_dropped.append(jnp.minimum(unlisted, SPARE))
+            unlisted += 1 - hit
+        hits.append(panel_hits)
+        kept.append(panel_kept)
+        dropped.append(panel_dropped)
+
+    def weight(panel, block, shift):
+        same = (dropped[panel][block] == shift).astype(jnp.int32)
+        return (same * kept[panel][block]).astype(F32)
+
+    def placed(panel, block):
+        parts = [
+            weight(panel, block, shift) * summed[panel, block - shift]
+            for shift in range(SPARE + 1)
+            if 0 <= block - shift < MOST
+        ]
+        return functools.reduce(jnp.add, parts)
+
+    for panel, source in enumerate((late_ref, early_ref)):
+        for block in range(blocks):
+            masked[block, :, panel * WIDTH : (panel + 1) * WIDTH] = (
+                source[block].astype(F32) * hits[panel][block]
+            ).astype(BF16)
+
+    pl.semaphore_wait(barrier, GRID_ROWS * GRID_COLS - 1)
+
+    def remote(source, target, send, recv, device):
+        return pltpu.make_async_remote_copy(
+            src_ref=source,
+            dst_ref=target,
+            send_sem=send,
+            recv_sem=recv,
+            device_id=device,
+            device_id_type=MESH,
+        )
+
+    def lanes(of_row):
+        return pl.ds(pl.multiple_of(of_row * LANES, LANES), LANES)
+
+    def first_copy(quarter, y_to):
+        return remote(
+            masked.at[y_to * half : (y_to + 1) * half, :, quarter * LANES : (quarter + 1) * LANES],
+            columns.at[:, col_id, :, quarter * LANES : (quarter + 1) * LANES],
+            first_send.at[quarter * 2 + y_to],
+            first_recv.at[col_id],
+            (jnp.int32(quarter), row_id * 2 + y_to),
+        )
+
+    def own_copy(quarter, y_to):
+        return pltpu.make_async_copy(
+            masked.at[y_to * half : (y_to + 1) * half, :, quarter * LANES : (quarter + 1) * LANES],
+            columns.at[:, col_id, :, quarter * LANES : (quarter + 1) * LANES],
+            first_recv.at[col_id],
+        )
+
+    def is_self(quarter, y_to):
+        return (row_id == quarter) & (col_id == row_id * 2 + y_to)
+
+    for quarter in range(GRID_ROWS):
+        for y_to in range(2):
+            pl.when(jnp.logical_not(is_self(quarter, y_to)))(first_copy(quarter, y_to).start)
+            pl.when(is_self(quarter, y_to))(own_copy(quarter, y_to).start)
+
+    def strip(source, of_row):
+        return columns.at[:, source, :, lanes(of_row)]
+
+    def core_copy(source):
+        part = strip(source, row_id)
+        return remote(part, part, core_send.at[source], core_recv.at[source], (core_peer, col_id))
+
+    def x_copy(source):
+        part = strip(source, row_id)
+        return remote(part, part, x_send.at[source], x_recv.at[source], (x_peer, col_id))
+
+    def relay_copy(source):
+        part = strip(source, x_peer)
+        return remote(part, part, relay_send.at[source], relay_recv.at[source], (core_peer, col_id))
+
+    def arrived(part, sem):
+        pltpu.make_async_copy(part, part, sem).wait()
+
+    for source in range(GRID_COLS):
+        arrived(strip(source, row_id), first_recv.at[source])
+        x_copy(source).start()
+        core_copy(source).start()
+    for source in range(GRID_COLS):
+        arrived(strip(source, x_peer), x_recv.at[source])
+        relay_copy(source).start()
+    core_other = lax.rem(core_peer + 2, GRID_ROWS)
+    for source in range(GRID_COLS):
+        arrived(strip(source, core_peer), core_recv.at[source])
+        arrived(strip(source, core_other), relay_recv.at[source])
+    inverse_copy.wait()
+
+    def y_copy(panel, step):
+        z_to = lax.rem(z_id + step, DEPTH)
+        return remote(
+            product.at[panel, :, z_to * 2 + 1 - y_id],
+            from_y.at[panel, step],
+            y_send.at[panel * DEPTH + step],
+            y_recv.at[panel * DEPTH + step],
+            (row_id, z_id * 2 + 1 - y_id),
+        )
+
+    def z_copy(panel, step):
+        z_to = lax.rem(z_id + step, DEPTH)
+        return remote(
+            to_z.at[panel, step],
+            from_z.at[panel, step],
+            z_send.at[panel * DEPTH + step],
+            z_recv.at[panel * DEPTH + step],
+            (row_id, z_to * 2 + y_id),
+        )
+
+    order = (1, 2, 3, 0)
+    for panel in range(2):
+        right = columns[:, :, :, panel * WIDTH : (panel + 1) * WIDTH].reshape(-1, WIDTH)
+        for start in range(0, blocks * BLK, 2 * BLK):
+            wide[start : start + 2 * BLK] = jnp.dot(
+                inverse[start : start + 2 * BLK], right, preferred_element_type=F32
+            )
+        for slot in range(MOST):
+            chosen = functools.reduce(
+                jnp.add,
+                [
+                    weight(panel, slot + shift, shift)
+                    * wide[(slot + shift) * BLK : (slot + shift + 1) * BLK]
+                    for shift in range(SPARE + 1)
+                ],
+            )
+            product[panel, slot] = chosen.astype(BF16).reshape(GRID_COLS, rows, WIDTH)
+        for step in order:
+            y_copy(panel, step).start()
+
+    for panel in range(2):
+        for step in order[:-1]:
+            y_copy(panel, step).wait_recv()
+            z_to = lax.rem(z_id + step, DEPTH)
+            to_z[panel, step] = (
+                product[panel, :, z_to * 2 + y_id].astype(F32) + from_y[panel, step].astype(F32)
+            ).astype(BF16)
+            z_copy(panel, step).start()
+
+    def finish(panel):
+        y_copy(panel, 0).wait_recv()
+        total = product[panel, :, z_id * 2 + y_id].astype(F32) + from_y[panel, 0].astype(F32)
+        for step in range(1, DEPTH):
+            z_copy(panel, step).wait_recv()
+            total += from_z[panel, step].astype(F32)
+        summed[panel] = total
+
+    place_id = row_id * 2 + y_id
+    peers = GRID_ROWS * 2
+    piece = (2 * WIDTH // peers, WIDTH // peers)
+    base = (0, 2 * WIDTH)
+
+    def plane_device(step):
+        other = lax.rem(place_id + step, peers)
+        return other, (other // 2, z_id * 2 + lax.rem(other, 2))
+
+    def part_of(stage, index):
+        size = piece[stage]
+        return pl.ds(pl.multiple_of(base[stage] + index * size, size), size)
+
+    def plane_copy(stage, step):
+        other, device = plane_device(step)
+        return remote(
+            sums.at[part_of(stage, other)],
+            plane_in.at[step, base[stage] // peers : base[stage] // peers + piece[stage]],
+            plane_send.at[stage * peers + step],
+            plane_recv.at[stage * peers + step],
+            device,
+        )
+
+    def depth_copy(stage, step):
+        z_to = lax.rem(z_id + step, DEPTH)
+        part = depth_in.at[z_id, base[stage] // peers : base[stage] // peers + piece[stage]]
+        return remote(
+            part,
+            part,
+            depth_send.at[stage * DEPTH + step],
+            depth_recv.at[stage * DEPTH + step],
+            (row_id, z_to * 2 + y_id),
+        )
+
+    def total_copy(stage, step):
+        _, device = plane_device(step)
+        part = totals.at[part_of(stage, place_id)]
+        return remote(
+            part,
+            part,
+            total_send.at[stage * peers + step],
+            total_recv.at[stage * peers + step],
+            device,
+        )
+
+    def store_sums(stage, value, at):
+        sums_wide[at : at + WIDTH] = value
+        sums[at : at + WIDTH] = value.astype(BF16)
+
+    def plane_sum(stage):
+        start = base[stage] // peers
+        total = sums_wide[part_of(stage, place_id)]
+        for step in range(1, peers):
+            plane_copy(stage, step).wait_recv()
+            total += plane_in[step, start : start + piece[stage]].astype(F32)
+        depth_in[z_id, start : start + piece[stage]] = total.astype(BF16)
+        for step in range(1, DEPTH):
+            depth_copy(stage, step).start()
+
+    def depth_sum(stage):
+        start = base[stage] // peers
+        for step in range(1, DEPTH):
+            source = lax.rem(z_id + DEPTH - step, DEPTH)
+            arrived(
+                depth_in.at[source, start : start + piece[stage]],
+                depth_recv.at[stage * DEPTH + step],
+            )
+        total = depth_in[0, start : start + piece[stage]].astype(F32)
+        for source in range(1, DEPTH):
+            total += depth_in[source, start : start + piece[stage]].astype(F32)
+        totals[part_of(stage, place_id)] = total.astype(BF16)
+        for step in range(1, peers):
+            total_copy(stage, step).start()
+
+    def gather_totals(stage):
+        for step in range(1, peers):
+            source = lax.rem(place_id + peers - step, peers)
+            arrived(totals.at[part_of(stage, source)], total_recv.at[stage * peers + step])
+
+    link = link_ref[...]
+    late_rows = masked[:, :, :WIDTH].reshape(-1, WIDTH)
+    early_rows = masked[:, :, WIDTH:].reshape(-1, WIDTH)
+
+    finish(0)
+    for block in range(blocks):
+        panel_late_ref[block] = -(placed(0, block) * hits[0][block])
+    late_flat = panel_late_ref[...].reshape(-1, WIDTH)
+    upper, lower = split_parts(late_flat)
+    store_sums(0, turned(late_rows, upper) + turned(late_rows, lower), 0)
+    store_sums(0, turned(upper, early_rows) + turned(lower, early_rows), WIDTH)
+    for step in range(1, peers):
+        plane_copy(0, step).start()
+    carried = jnp.dot(upper, link, preferred_element_type=F32) + jnp.dot(
+        lower, link, preferred_element_type=F32
+    )
+    carried = carried.reshape(blocks, rows, WIDTH)
+
+    finish(1)
+    for block in range(blocks):
+        panel_early_ref[block] = -(
+            (placed(1, block) + carried[block]) * hits[1][block]
+        )
+    early_upper, early_lower = split_parts(panel_early_ref[...].reshape(-1, WIDTH))
+    store_sums(1, turned(early_rows, early_upper) + turned(early_rows, early_lower), 2 * WIDTH)
+    for step in range(1, peers):
+        plane_copy(1, step).start()
+
+    plane_sum(0)
+    plane_sum(1)
+    depth_sum(0)
+    depth_sum(1)
+    gather_totals(0)
+    diag_late = diag_ref[0] - totals[:WIDTH].astype(F32)
+    diag_late_ref[...] = diag_late
+    upper, lower = split_parts(diag_late)
+    cross = (
+        -totals[WIDTH : 2 * WIDTH].astype(F32)
+        - jnp.dot(upper, link, preferred_element_type=F32)
+        - jnp.dot(lower, link, preferred_element_type=F32)
+    )
+    cross_ref[...] = cross
+    upper, lower = split_parts(cross)
+    carried = turned(link, upper) + turned(link, lower)
+    gather_totals(1)
+    diag_early_ref[...] = diag_ref[1] - totals[2 * WIDTH :].astype(F32) - carried
+
+    for quarter in range(GRID_ROWS):
+        for y_to in range(2):
+            pl.when(jnp.logical_not(is_self(quarter, y_to)))(first_copy(quarter, y_to).wait_send)
+    for source in range(GRID_COLS):
+        x_copy(source).wait_send()
+        core_copy(source).wait_send()
+        relay_copy(source).wait_send()
+    for panel in range(2):
+        for step in range(DEPTH):
+            y_copy(panel, step).wait_send()
+        for step in range(1, DEPTH):
+            z_copy(panel, step).wait_send()
+            depth_copy(panel, step).wait_send()
+        for step in range(1, peers):
+            plane_copy(panel, step).wait_send()
+            total_copy(panel, step).wait_send()
+
+
+def kernel_shards(inverse_blocks, lower_late, lower_early, link_block, diag_inverse, structures):
+    blocks, rows, _ = lower_late.shape
+    dma = pltpu.SemaphoreType.DMA
+    vmem = pl.BlockSpec(memory_space=pltpu.VMEM)
+    square = jax.ShapeDtypeStruct((WIDTH, WIDTH), F32)
+    panel = jax.ShapeDtypeStruct(lower_late.shape, F32)
+    peers = GRID_ROWS * 2
+    sized = pltpu.VMEM
+    return pl.pallas_call(
+        step_kernel,
+        out_shape=(panel, square, panel, square, square),
+        in_specs=[
+            pl.BlockSpec(memory_space=pl.ANY),
+            vmem,
+            vmem,
+            vmem,
+            vmem,
+            pl.BlockSpec(memory_space=pltpu.SMEM),
+        ],
+        out_specs=(vmem,) * 5,
+        scratch_shapes=[
+            sized(inverse_blocks.shape, BF16),
+            sized((blocks, rows, 2 * WIDTH), BF16),
+            sized((blocks // 2, GRID_COLS, rows, 2 * WIDTH), BF16),
+            sized((blocks * BLK, WIDTH), F32),
+            sized((2, MOST, GRID_COLS, rows, WIDTH), BF16),
+            sized((2, DEPTH, MOST, rows, WIDTH), BF16),
+            sized((2, DEPTH, MOST, rows, WIDTH), BF16),
+            sized((2, DEPTH, MOST, rows, WIDTH), BF16),
+            sized((2, MOST, rows, WIDTH), F32),
+            sized((3 * WIDTH, WIDTH), BF16),
+            sized((3 * WIDTH, WIDTH), F32),
+            sized((peers, 3 * WIDTH // peers, WIDTH), BF16),
+            sized((DEPTH, 3 * WIDTH // peers, WIDTH), BF16),
+            sized((3 * WIDTH, WIDTH), BF16),
+            dma,
+            dma((GRID_ROWS * 2,)),
+            dma((GRID_COLS,)),
+            dma((GRID_COLS,)),
+            dma((GRID_COLS,)),
+            dma((GRID_COLS,)),
+            dma((GRID_COLS,)),
+            dma((GRID_COLS,)),
+            dma((GRID_COLS,)),
+            dma((2 * DEPTH,)),
+            dma((2 * DEPTH,)),
+            dma((2 * DEPTH,)),
+            dma((2 * DEPTH,)),
+            dma((2 * peers,)),
+            dma((2 * peers,)),
+            dma((2 * DEPTH,)),
+            dma((2 * DEPTH,)),
+            dma((2 * peers,)),
+            dma((2 * peers,)),
+        ],
+        compiler_params=pltpu.CompilerParams(
+            collective_id=0, has_side_effects=True, vmem_limit_bytes=40 * 1024 * 1024
+        ),
+    )(inverse_blocks, lower_late, lower_early, link_block, diag_inverse, structures)
+
+
 def solution(mesh):
     placed = (P("prow", "pcol"), P("prow", "pcol", None), P("prow", "pcol", None), P(), P(), P())
+
+    def shards(inverse_blocks, lower_late, *others):
+        if fits_kernel(mesh, inverse_blocks, lower_late):
+            return kernel_shards(inverse_blocks, lower_late, *others)
+        return plain_shards(inverse_blocks, lower_late, *others)
+
     return jax.shard_map(
         shards,
         mesh=mesh,

time: 406 us -> 69.6 us (0.17)
  waiting for transfers between devices: 289 us -> 0 us
  blocking collectives: 70.5 us -> 0 us
  Pallas kernels: 0 us -> 58.9 us
  matrix products: 16.6 us -> 0 us
  between operations: 13.9 us -> 0.66 us
  other arithmetic: 9.06 us -> 0 us
    psum x2 -> x0, waiting for transfers between devices: 168 us -> none  [the longest x1 131 us: shards(): sum_late = lax.psum(local_late, ('prow', 'pcol'))]
    reduce_scatter x2 -> x0, waiting for transfers between devices: 121 us -> none  [reduce_columns(): lax.psum_scatter(product.reshape(row_blocks, BLK, count * WIDTH).astype(j...]
    all_gather x2 -> x0, blocking collectives: 70.5 us -> none  [separate_reduce(): strip = lax.all_gather(masked, 'pcol', axis=1, tiled=True)]
    pallas_call x0 -> x1, Pallas kernels: none -> 58.9 us  [kernel_shards(): pl.pallas_call(step_kernel, out_shape=(panel, square, panel, square, squa...]
    dot_general x12 -> x0, matrix products: 16.6 us -> none  [the longest x2 6.28 us: reduce_columns(): jnp.dot(inverse_blocks, columns, preferred_element_type=jnp.float32)]
    unnamed x22 -> x17, local copies, waits for them, and re-layouts: 0.71 us -> 9.8 us
    convert_element_type x2 -> x0, local copies, waits for them, and re-layouts: 4.47 us -> none  [reduce_columns(): product.reshape(row_blocks, BLK, count * WIDTH).astype(jnp.bfloat16)]
  transfers between devices with their start and end apart: 4 -> 0, of which waited for: 4 -> 0; matrix products, arithmetic and copies ran while one was open for 3% -> 0% of each run, Pallas kernels for 0% -> 0%
where the time goes in v1:
time: 69.6 us; the launch traced here: 69.3 us
  Pallas kernels  58.9 us (85%)
  local copies, waits for them, and re-layouts  9.8 us (14%)
    pallas_call x1, Pallas kernels, kernel_shards(): pl.pallas_call(step_kernel, out_shape=(panel, square, panel, square, squa...  58.9 us
    unnamed x17, local copies, waits for them, and re-layouts  9.8 us

profile of v1, /device:TPU:0, one launch (start us, length us, event | category | flops | bytes accessed | tf_op | source)
XLA Modules:
  0.0 69.3 jit_solution(11711953329812643337)
XLA Ops:
  0.6 0.0 copy-start
  0.6 1.9 %copy-done = bf16[1792,896]{1,0:T(8,128)(2,1)S(1)} copy-done((bf16[1792,896]{1,0:T(8,128)(2,1)S(1)}, bf16[1792,896]{1,0:T(8,128)(2,1)}, u32[]{:S(2)}) %copy-start) | copy-done | bytes 3211288
  2.5 0.0 copy-start.1
  2.5 1.0 %copy-done.1 = f32[2,256,256]{2,1,0:T(8,128)S(1)} copy-done((f32[2,256,256]{2,1,0:T(8,128)S(1)}, f32[2,256,256]{2,1,0:T(8,128)}, u32[]{:S(2)}) %copy-start.1) | copy-done | bytes 524312
  3.6 0.0 copy-start.2
  3.6 0.9 %copy-done.2 = bf16[256,256]{1,0:T(8,128)(2,1)S(1)} copy-done((bf16[256,256]{1,0:T(8,128)(2,1)S(1)}, bf16[256,256]{1,0:T(8,128)(2,1)}, u32[]{:S(2)}) %copy-start.2) | copy-done | bytes 131096
  4.5 0.0 copy-start.3
  4.5 0.9 %copy-done.3 = bf16[14,16,256]{2,1,0:T(8,128)(2,1)S(1)} copy-done((bf16[14,16,256]{2,1,0:T(8,128)(2,1)S(1)}, bf16[14,16,256]{2,1,0:T(8,128)(2,1)}, u32[]{:S(2)}) %copy-start.3) | copy-done | bytes 114712
  5.4 0.0 copy-start.4
  5.4 0.9 %copy-done.4 = bf16[14,16,256]{2,1,0:T(8,128)(2,1)S(1)} copy-done((bf16[14,16,256]{2,1,0:T(8,128)(2,1)S(1)}, bf16[14,16,256]{2,1,0:T(8,128)(2,1)}, u32[]{:S(2)}) %copy-start.4) | copy-done | bytes 114712
  6.3 0.0 copy-start.5
  6.3 0.7 copy-done.5
  7.0 58.9 %shard_map.101 = (f32[14,16,256]{2,1,0:T(8,128)S(1)}, f32[256,256]{1,0:T(8,128)S(1)}, f32[14,16,256]{2,1,0:T(8,128)S(1)}, f32[256,256]{1,0:T(8,128)S(1)}, f32[256,256]{1,0:T(8,128)S(1)}) custom-call(bf16[1792,896]{1,0:T(8,128)(2,1)S(1)} %copy-done, bf16[14,16,256]{2,1,0:T(8,128)(2,1)S(1)} %copy-done.3, bf16[14,16,256]{2,1,0:T(8,128)(2,1)S(1)} %copy-done.4, ...), custom_call_target="tpu_custom_call" | custom-call | tf_op jit(solution)/shard_map/pallas_call | solution.py:464
  65.9 0.7 copy.16
  66.5 0.7 %copy.17 = f32[256,256]{1,0:T(8,128)} copy(f32[256,256]{1,0:T(8,128)S(1)} %get-tuple-element.11) | data formatting | bytes 524288
  67.2 0.7 copy.18
  67.9 0.7 %copy.19 = f32[256,256]{1,0:T(8,128)} copy(f32[256,256]{1,0:T(8,128)S(1)} %get-tuple-element.13) | data formatting | bytes 524288
  68.6 0.7 %copy.20 = f32[256,256]{1,0:T(8,128)} copy(f32[256,256]{1,0:T(8,128)S(1)} %get-tuple-element.14) | data formatting | bytes 524288
Async XLA Ops:
  0.6 1.9 %copy-start = (bf16[1792,896]{1,0:T(8,128)(2,1)S(1)}, bf16[1792,896]{1,0:T(8,128)(2,1)}, u32[]{:S(2)}) copy-start(bf16[1792,896]{1,0:T(8,128)(2,1)} %inverse_hbm.1) | copy-start | bytes 9633796
  2.5 1.0 %copy-start.1 = (f32[2,256,256]{2,1,0:T(8,128)S(1)}, f32[2,256,256]{2,1,0:T(8,128)}, u32[]{:S(2)}) copy-start(f32[2,256,256]{2,1,0:T(8,128)} %diag_ref.1) | copy-start | bytes 1572868
  3.6 0.9 %copy-start.2 = (bf16[256,256]{1,0:T(8,128)(2,1)S(1)}, bf16[256,256]{1,0:T(8,128)(2,1)}, u32[]{:S(2)}) copy-start(bf16[256,256]{1,0:T(8,128)(2,1)} %link_ref.1) | copy-start | bytes 393220
  4.5 0.9 %copy-start.3 = (bf16[14,16,256]{2,1,0:T(8,128)(2,1)S(1)}, bf16[14,16,256]{2,1,0:T(8,128)(2,1)}, u32[]{:S(2)}) copy-start(bf16[14,16,256]{2,1,0:T(8,128)(2,1)} %late_ref.1) | copy-start | bytes 344068
  5.4 0.9 %copy-start.4 = (bf16[14,16,256]{2,1,0:T(8,128)(2,1)S(1)}, bf16[14,16,256]{2,1,0:T(8,128)(2,1)}, u32[]{:S(2)}) copy-start(bf16[14,16,256]{2,1,0:T(8,128)(2,1)} %early_ref.1) | copy-start | bytes 344068
  6.3 0.7 copy-start.5

commit v2 on v1

--- a/solution.py
+++ b/solution.py
@@ -114,11 +114,11 @@
 
 
 def step_kernel(
-    inverse_hbm, late_ref, early_ref, link_ref, diag_ref, structures_ref,
+    inverse_hbm, late_hbm, early_hbm, link_hbm, diag_hbm, structures_ref,
     panel_late_ref, diag_late_ref, panel_early_ref, cross_ref, diag_early_ref,
-    inverse, masked, columns, wide, product, from_y, to_z, from_z, summed,
+    inverse, late_ref, early_ref, link_ref, diag_ref, masked, columns, wide, product, from_y, to_z, from_z, summed,
     sums, sums_wide, plane_in, depth_in, totals,
-    inverse_sem, first_send, first_recv, core_send, core_recv, x_send, x_recv,
+    late_sem, early_sem, inverse_sem, link_sem, diag_sem, first_send, first_recv, core_send, core_recv, x_send, x_recv,
     relay_send, relay_recv, y_send, y_recv, z_send, z_recv,
     plane_send, plane_recv, depth_send, depth_recv, total_send, total_recv,
 ):
@@ -132,8 +132,13 @@
     core_peer = row_id + 1 - 2 * lax.rem(row_id, 2)
     x_peer = lax.rem(row_id + 2, GRID_ROWS)
 
+    late_copy = pltpu.make_async_copy(late_hbm, late_ref, late_sem)
+    early_copy = pltpu.make_async_copy(early_hbm, early_ref, early_sem)
     inverse_copy = pltpu.make_async_copy(inverse_hbm, inverse, inverse_sem)
-    inverse_copy.start()
+    link_copy = pltpu.make_async_copy(link_hbm, link_ref, link_sem)
+    diag_copy = pltpu.make_async_copy(diag_hbm, diag_ref, diag_sem)
+    for copy in (late_copy, early_copy, inverse_copy, link_copy, diag_copy):
+        copy.start()
 
     barrier = pltpu.get_barrier_semaphore()
     for step in range(1, GRID_ROWS * GRID_COLS):
@@ -145,41 +150,23 @@
             device_id_type=MESH,
         )
 
-    hits, kept, dropped = [], [], []
+    hits = []
     for panel in range(2):
-        lowest = row_id * blocks
-        entries = [structures_ref[panel, entry] - lowest for entry in range(listed)]
-        unlisted = jnp.int32(0)
-        panel_hits, panel_kept, panel_dropped = [], [], []
+        entries = [structures_ref[panel, entry] - row_id * blocks for entry in range(listed)]
+        panel_hits = []
         for block in range(blocks):
             hit = jnp.int32(0)
             for entry in entries:
                 hit += (entry == block).astype(jnp.int32)
-            drop = (1 - hit) * (unlisted < SPARE).astype(jnp.int32)
-            panel_hits.append(hit.astype(F32))
-            panel_kept.append(1 - drop)
-            panel_dropped.append(jnp.minimum(unlisted, SPARE))
-            unlisted += 1 - hit
+            panel_hits.append(hit)
         hits.append(panel_hits)
-        kept.append(panel_kept)
-        dropped.append(panel_dropped)
-
-    def weight(panel, block, shift):
-        same = (dropped[panel][block] == shift).astype(jnp.int32)
-        return (same * kept[panel][block]).astype(F32)
-
-    def placed(panel, block):
-        parts = [
-            weight(panel, block, shift) * summed[panel, block - shift]
-            for shift in range(SPARE + 1)
-            if 0 <= block - shift < MOST
-        ]
-        return functools.reduce(jnp.add, parts)
-
+
+    late_copy.wait()
+    early_copy.wait()
     for panel, source in enumerate((late_ref, early_ref)):
         for block in range(blocks):
             masked[block, :, panel * WIDTH : (panel + 1) * WIDTH] = (
-                source[block].astype(F32) * hits[panel][block]
+                source[block].astype(F32) * hits[panel][block].astype(F32)
             ).astype(BF16)
 
     pl.semaphore_wait(barrier, GRID_ROWS * GRID_COLS - 1)
@@ -194,63 +181,98 @@
             device_id_type=MESH,
         )
 
-    def lanes(of_row):
-        return pl.ds(pl.multiple_of(of_row * LANES, LANES), LANES)
-
-    def first_copy(quarter, y_to):
-        return remote(
-            masked.at[y_to * half : (y_to + 1) * half, :, quarter * LANES : (quarter + 1) * LANES],
-            columns.at[:, col_id, :, quarter * LANES : (quarter + 1) * LANES],
-            first_send.at[quarter * 2 + y_to],
-            first_recv.at[col_id],
-            (jnp.int32(quarter), row_id * 2 + y_to),
-        )
-
-    def own_copy(quarter, y_to):
-        return pltpu.make_async_copy(
-            masked.at[y_to * half : (y_to + 1) * half, :, quarter * LANES : (quarter + 1) * LANES],
-            columns.at[:, col_id, :, quarter * LANES : (quarter + 1) * LANES],
-            first_recv.at[col_id],
-        )
-
-    def is_self(quarter, y_to):
-        return (row_id == quarter) & (col_id == row_id * 2 + y_to)
-
-    for quarter in range(GRID_ROWS):
-        for y_to in range(2):
-            pl.when(jnp.logical_not(is_self(quarter, y_to)))(first_copy(quarter, y_to).start)
-            pl.when(is_self(quarter, y_to))(own_copy(quarter, y_to).start)
-
-    def strip(source, of_row):
-        return columns.at[:, source, :, lanes(of_row)]
-
-    def core_copy(source):
-        part = strip(source, row_id)
-        return remote(part, part, core_send.at[source], core_recv.at[source], (core_peer, col_id))
-
-    def x_copy(source):
-        part = strip(source, row_id)
-        return remote(part, part, x_send.at[source], x_recv.at[source], (x_peer, col_id))
-
-    def relay_copy(source):
-        part = strip(source, x_peer)
-        return remote(part, part, relay_send.at[source], relay_recv.at[source], (core_peer, col_id))
+    core_id = lax.rem(row_id, 2)
+    x_id = row_id // 2
+
+    def strip(panel, source, x_half):
+        start = pl.multiple_of(panel * WIDTH + x_half * LANES, LANES)
+        return columns.at[:, source, :, pl.ds(start, LANES)]
+
+    def first_parts(panel, x_half, y_to):
+        start = panel * WIDTH + x_half * LANES
+        part = masked.at[y_to * half : (y_to + 1) * half, :, start : start + LANES]
+        target = (x_half * 2 + lax.rem(y_id + panel, 2), row_id * 2 + y_to)
+        at_self = (row_id == target[0]) & (col_id == target[1])
+        return part, strip(panel, col_id, x_half), target, at_self
+
+    def first_copy(panel, x_half, y_to):
+        part, to, target, _ = first_parts(panel, x_half, y_to)
+        send = first_send.at[panel * 4 + x_half * 2 + y_to]
+        return remote(part, to, send, first_recv.at[panel * DEPTH + z_id], target)
+
+    def own_copy(panel, x_half, y_to):
+        part, to, _, _ = first_parts(panel, x_half, y_to)
+        return pltpu.make_async_copy(part, to, first_recv.at[panel * DEPTH + z_id])
+
+    def is_self(panel, x_half, y_to):
+        return first_parts(panel, x_half, y_to)[3]
+
+    first_cases = [(p, x, y) for p in range(2) for x in range(2) for y in range(2)]
+    for case in first_cases:
+        pl.when(jnp.logical_not(is_self(*case)))(first_copy(*case).start)
+        pl.when(is_self(*case))(own_copy(*case).start)
+
+    def here(panel, index):
+        return index * 2 + lax.rem(core_id + panel, 2)
+
+    def there(panel, index):
+        return index * 2 + lax.rem(core_id + panel + 1, 2)
+
+    def core_copy(panel, index):
+        part, at = strip(panel, here(panel, index), x_id), panel * DEPTH + index
+        return remote(part, part, core_send.at[at], core_recv.at[at], (core_peer, col_id))
+
+    def x_copy(panel, index):
+        part, at = strip(panel, here(panel, index), x_id), panel * DEPTH + index
+        return remote(part, part, x_send.at[at], x_recv.at[at], (x_peer, col_id))
+
+    def relay_copy(panel, index):
+        part, at = strip(panel, here(panel, index), 1 - x_id), panel * DEPTH + index
+        return remote(part, part, relay_send.at[at], relay_recv.at[at], (core_peer, col_id))
 
     def arrived(part, sem):
         pltpu.make_async_copy(part, part, sem).wait()
 
-    for source in range(GRID_COLS):
-        arrived(strip(source, row_id), first_recv.at[source])
-        x_copy(source).start()
-        core_copy(source).start()
-    for source in range(GRID_COLS):
-        arrived(strip(source, x_peer), x_recv.at[source])
-        relay_copy(source).start()
-    core_other = lax.rem(core_peer + 2, GRID_ROWS)
-    for source in range(GRID_COLS):
-        arrived(strip(source, core_peer), core_recv.at[source])
-        arrived(strip(source, core_other), relay_recv.at[source])
-    inverse_copy.wait()
+    def spread(panel):
+        for index in range(DEPTH):
+            arrived(strip(panel, here(panel, index), x_id), first_recv.at[panel * DEPTH + index])
+            x_copy(panel, index).start()
+            core_copy(panel, index).start()
+
+    def relay(panel):
+        for index in range(DEPTH):
+            arrived(strip(panel, here(panel, index), 1 - x_id), x_recv.at[panel * DEPTH + index])
+            relay_copy(panel, index).start()
+
+    def collect(panel):
+        for index in range(DEPTH):
+            at = panel * DEPTH + index
+            arrived(strip(panel, there(panel, index), x_id), core_recv.at[at])
+            arrived(strip(panel, there(panel, index), 1 - x_id), relay_recv.at[at])
+
+    kept, dropped = [], []
+    for panel in range(2):
+        unlisted = jnp.int32(0)
+        panel_kept, panel_dropped = [], []
+        for block in range(blocks):
+            drop = (1 - hits[panel][block]) * (unlisted < SPARE).astype(jnp.int32)
+            panel_kept.append(1 - drop)
+            panel_dropped.append(jnp.minimum(unlisted, SPARE))
+            unlisted += 1 - hits[panel][block]
+        kept.append(panel_kept)
+        dropped.append(panel_dropped)
+
+    def weight(panel, block, shift):
+        same = (dropped[panel][block] == shift).astype(jnp.int32)
+        return (same * kept[panel][block]).astype(F32)
+
+    def placed(panel, block):
+        parts = [
+            weight(panel, block, shift) * summed[panel, block - shift]
+            for shift in range(SPARE + 1)
+            if 0 <= block - shift < MOST
+        ]
+        return functools.reduce(jnp.add, parts)
 
     def y_copy(panel, step):
         z_to = lax.rem(z_id + step, DEPTH)
@@ -273,7 +295,8 @@
         )
 
     order = (1, 2, 3, 0)
-    for panel in range(2):
+
+    def multiply(panel):
         right = columns[:, :, :, panel * WIDTH : (panel + 1) * WIDTH].reshape(-1, WIDTH)
         for start in range(0, blocks * BLK, 2 * BLK):
             wide[start : start + 2 * BLK] = jnp.dot(
@@ -292,14 +315,13 @@
         for step in order:
             y_copy(panel, step).start()
 
-    for panel in range(2):
-        for step in order[:-1]:
-            y_copy(panel, step).wait_recv()
-            z_to = lax.rem(z_id + step, DEPTH)
-            to_z[panel, step] = (
-                product[panel, :, z_to * 2 + y_id].astype(F32) + from_y[panel, step].astype(F32)
-            ).astype(BF16)
-            z_copy(panel, step).start()
+    def forward(panel, step):
+        y_copy(panel, step).wait_recv()
+        z_to = lax.rem(z_id + step, DEPTH)
+        to_z[panel, step] = (
+            product[panel, :, z_to * 2 + y_id].astype(F32) + from_y[panel, step].astype(F32)
+        ).astype(BF16)
+        z_copy(panel, step).start()
 
     def finish(panel):
         y_copy(panel, 0).wait_recv()
@@ -388,13 +410,28 @@
             source = lax.rem(place_id + peers - step, peers)
             arrived(totals.at[part_of(stage, source)], total_recv.at[stage * peers + step])
 
+    link_copy.wait()
+    diag_copy.wait()
     link = link_ref[...]
     late_rows = masked[:, :, :WIDTH].reshape(-1, WIDTH)
     early_rows = masked[:, :, WIDTH:].reshape(-1, WIDTH)
 
+    spread(0)
+    relay(0)
+    collect(0)
+    inverse_copy.wait()
+    multiply(0)
+    spread(1)
+    forward(0, 1)
+    relay(1)
+    forward(0, 2)
+    collect(1)
+    multiply(1)
+    forward(0, 3)
+
     finish(0)
     for block in range(blocks):
-        panel_late_ref[block] = -(placed(0, block) * hits[0][block])
+        panel_late_ref[block] = -(placed(0, block) * hits[0][block].astype(F32))
     late_flat = panel_late_ref[...].reshape(-1, WIDTH)
     upper, lower = split_parts(late_flat)
     store_sums(0, turned(late_rows, upper) + turned(late_rows, lower), 0)
@@ -406,19 +443,22 @@
     )
     carried = carried.reshape(blocks, rows, WIDTH)
 
+    for step in order[:-1]:
+        forward(1, step)
+    plane_sum(0)
+
     finish(1)
     for block in range(blocks):
         panel_early_ref[block] = -(
-            (placed(1, block) + carried[block]) * hits[1][block]
+            (placed(1, block) + carried[block]) * hits[1][block].astype(F32)
         )
     early_upper, early_lower = split_parts(panel_early_ref[...].reshape(-1, WIDTH))
     store_sums(1, turned(early_rows, early_upper) + turned(early_rows, early_lower), 2 * WIDTH)
     for step in range(1, peers):
         plane_copy(1, step).start()
 
-    plane_sum(0)
+    depth_sum(0)
     plane_sum(1)
-    depth_sum(0)
     depth_sum(1)
     gather_totals(0)
     diag_late = diag_ref[0] - totals[:WIDTH].astype(F32)
@@ -435,13 +475,13 @@
     gather_totals(1)
     diag_early_ref[...] = diag_ref[1] - totals[2 * WIDTH :].astype(F32) - carried
 
-    for quarter in range(GRID_ROWS):
-        for y_to in range(2):
-            pl.when(jnp.logical_not(is_self(quarter, y_to)))(first_copy(quarter, y_to).wait_send)
-    for source in range(GRID_COLS):
-        x_copy(source).wait_send()
-        core_copy(source).wait_send()
-        relay_copy(source).wait_send()
+    for case in first_cases:
+        pl.when(jnp.logical_not(is_self(*case)))(first_copy(*case).wait_send)
+    for panel in range(2):
+        for index in range(DEPTH):
+            x_copy(panel, index).wait_send()
+            core_copy(panel, index).wait_send()
+            relay_copy(panel, index).wait_send()
     for panel in range(2):
         for step in range(DEPTH):
             y_copy(panel, step).wait_send()
@@ -465,16 +505,16 @@
         step_kernel,
         out_shape=(panel, square, panel, square, square),
         in_specs=[
-            pl.BlockSpec(memory_space=pl.ANY),
-            vmem,
-            vmem,
-            vmem,
-            vmem,
+            *(pl.BlockSpec(memory_space=pl.ANY),) * 5,
             pl.BlockSpec(memory_space=pltpu.SMEM),
         ],
         out_specs=(vmem,) * 5,
         scratch_shapes=[
             sized(inverse_blocks.shape, BF16),
+            sized(lower_late.shape, BF16),
+            sized(lower_early.shape, BF16),
+            sized(link_block.shape, BF16),
+            sized(diag_inverse.shape, F32),
             sized((blocks, rows, 2 * WIDTH), BF16),
             sized((blocks // 2, GRID_COLS, rows, 2 * WIDTH), BF16),
             sized((blocks * BLK, WIDTH), F32),
@@ -489,6 +529,10 @@
             sized((DEPTH, 3 * WIDTH // peers, WIDTH), BF16),
             sized((3 * WIDTH, WIDTH), BF16),
             dma,
+            dma,
+            dma,
+            dma,
+            dma,
             dma((GRID_ROWS * 2,)),
             dma((GRID_COLS,)),
             dma((GRID_COLS,)),
@@ -509,7 +553,7 @@
             dma((2 * peers,)),
         ],
         compiler_params=pltpu.CompilerParams(
-            collective_id=0, has_side_effects=True, vmem_limit_bytes=40 * 1024 * 1024
+            collective_id=0, has_side_effects=True, vmem_limit_bytes=52 * 1024 * 1024
         ),
     )(inverse_blocks, lower_late, lower_early, link_block, diag_inverse, structures)
 

time: 69.6 us -> 68 us (0.977)
  local copies, waits for them, and re-layouts: 9.8 us -> 6.86 us
  Pallas kernels: 58.9 us -> 60.3 us
    unnamed x17 -> x13, local copies, waits for them, and re-layouts: 9.8 us -> 6.86 us
    pallas_call x1, Pallas kernels: 58.9 us -> 60.3 us  [kernel_shards(): pl.pallas_call(step_kernel, out_shape=(panel, square, panel, square, squa...]
where the time goes in v2:
time: 68 us; the launch traced here: 67.8 us
  Pallas kernels  60.3 us (89%)
  local copies, waits for them, and re-layouts  6.86 us (10%)
    pallas_call x1, Pallas kernels, kernel_shards(): pl.pallas_call(step_kernel, out_shape=(panel, square, panel, square, squa...  60.3 us
    unnamed x13, local copies, waits for them, and re-layouts  6.86 us

profile of v2, /device:TPU:0, one launch (start us, length us, event | category | flops | bytes accessed | tf_op | source)
XLA Modules:
  0.0 67.8 jit_solution(12051252004390941137)
XLA Ops:
  0.6 0.0 copy-start
  0.6 0.9 %copy-done = bf16[256,256]{1,0:T(8,128)(2,1)S(1)} copy-done((bf16[256,256]{1,0:T(8,128)(2,1)S(1)}, bf16[256,256]{1,0:T(8,128)(2,1)}, u32[]{:S(2)}) %copy-start) | copy-done | bytes 131096
  1.5 0.0 copy-start.1
  1.5 0.9 %copy-done.1 = bf16[14,16,256]{2,1,0:T(8,128)(2,1)S(1)} copy-done((bf16[14,16,256]{2,1,0:T(8,128)(2,1)S(1)}, bf16[14,16,256]{2,1,0:T(8,128)(2,1)}, u32[]{:S(2)}) %copy-start.1) | copy-done | bytes 114712
  2.4 0.0 copy-start.2
  2.4 0.9 %copy-done.2 = bf16[14,16,256]{2,1,0:T(8,128)(2,1)S(1)} copy-done((bf16[14,16,256]{2,1,0:T(8,128)(2,1)S(1)}, bf16[14,16,256]{2,1,0:T(8,128)(2,1)}, u32[]{:S(2)}) %copy-start.2) | copy-done | bytes 114712
  3.3 0.0 copy-start.3
  3.3 0.7 copy-done.3
  4.0 60.3 %shard_map.101 = (f32[14,16,256]{2,1,0:T(8,128)S(1)}, f32[256,256]{1,0:T(8,128)S(1)}, f32[14,16,256]{2,1,0:T(8,128)S(1)}, f32[256,256]{1,0:T(8,128)S(1)}, f32[256,256]{1,0:T(8,128)S(1)}) custom-call(bf16[1792,896]{1,0:T(8,128)(2,1)} %inverse_hbm.1, bf16[14,16,256]{2,1,0:T(8,128)(2,1)S(1)} %copy-done.1, bf16[14,16,256]{2,1,0:T(8,128)(2,1)S(1)} %copy-done.2, ...), custom_call_target="tpu_custom_call" | custom-call | tf_op jit(solution)/shard_map/pallas_call | solution.py:504
  64.3 0.7 %copy.16 = f32[14,16,256]{2,1,0:T(8,128)} copy(f32[14,16,256]{2,1,0:T(8,128)S(1)} %get-tuple-element.10) | data formatting | bytes 458752
  65.0 0.7 %copy.17 = f32[256,256]{1,0:T(8,128)} copy(f32[256,256]{1,0:T(8,128)S(1)} %get-tuple-element.11) | data formatting | bytes 524288
  65.7 0.7 %copy.18 = f32[14,16,256]{2,1,0:T(8,128)} copy(f32[14,16,256]{2,1,0:T(8,128)S(1)} %get-tuple-element.12) | data formatting | bytes 458752
  66.4 0.7 %copy.19 = f32[256,256]{1,0:T(8,128)} copy(f32[256,256]{1,0:T(8,128)S(1)} %get-tuple-element.13) | data formatting | bytes 524288
  67.1 0.7 %copy.20 = f32[256,256]{1,0:T(8,128)} copy(f32[256,256]{1,0:T(8,128)S(1)} %get-tuple-element.14) | data formatting | bytes 524288
Async XLA Ops:
  0.6 0.9 %copy-start = (bf16[256,256]{1,0:T(8,128)(2,1)S(1)}, bf16[256,256]{1,0:T(8,128)(2,1)}, u32[]{:S(2)}) copy-start(bf16[256,256]{1,0:T(8,128)(2,1)} %link_hbm.1) | copy-start | bytes 393220
  1.5 0.9 %copy-start.1 = (bf16[14,16,256]{2,1,0:T(8,128)(2,1)S(1)}, bf16[14,16,256]{2,1,0:T(8,128)(2,1)}, u32[]{:S(2)}) copy-start(bf16[14,16,256]{2,1,0:T(8,128)(2,1)} %late_hbm.1) | copy-start | bytes 344068
  2.4 0.9 %copy-start.2 = (bf16[14,16,256]{2,1,0:T(8,128)(2,1)S(1)}, bf16[14,16,256]{2,1,0:T(8,128)(2,1)}, u32[]{:S(2)}) copy-start(bf16[14,16,256]{2,1,0:T(8,128)(2,1)} %early_hbm.1) | copy-start | bytes 344068
  3.3 0.7 %copy-start.3 = (s32[2,28]{1,0:T(2,128)S(1)}, s32[2,28]{1,0:T(2,128)}, u32[]{:S(2)}) copy-start(s32[2,28]{1,0:T(2,128)} %structures_ref.1) | copy-start | bytes 676

commit v3 on v2

--- a/solution.py
+++ b/solution.py
@@ -428,6 +428,8 @@
     collect(1)
     multiply(1)
     forward(0, 3)
+    for step in order[:-1]:
+        forward(1, step)
 
     finish(0)
     for block in range(blocks):
@@ -443,8 +445,6 @@
     )
     carried = carried.reshape(blocks, rows, WIDTH)
 
-    for step in order[:-1]:
-        forward(1, step)
     plane_sum(0)
 
     finish(1)

time: 68 us -> 63.9 us (0.940)
  Pallas kernels: 60.3 us -> 56.2 us
    pallas_call x1, Pallas kernels: 60.3 us -> 56.2 us  [kernel_shards(): pl.pallas_call(step_kernel, out_shape=(panel, square, panel, square, squa...]
where the time goes in v3:
time: 63.9 us; the launch traced here: 63.7 us
  Pallas kernels  56.2 us (88%)
  local copies, waits for them, and re-layouts  6.86 us (11%)
  between operations  0.65 us (1%)
    pallas_call x1, Pallas kernels, kernel_shards(): pl.pallas_call(step_kernel, out_shape=(panel, square, panel, square, squa...  56.2 us
    unnamed x13, local copies, waits for them, and re-layouts  6.86 us

profile of v3, /device:TPU:0, one launch (start us, length us, event | category | flops | bytes accessed | tf_op | source)
XLA Modules:
  0.0 63.7 jit_solution(2382432551042733242)
XLA Ops:
  0.6 0.0 copy-start
  0.6 0.9 %copy-done = bf16[256,256]{1,0:T(8,128)(2,1)S(1)} copy-done((bf16[256,256]{1,0:T(8,128)(2,1)S(1)}, bf16[256,256]{1,0:T(8,128)(2,1)}, u32[]{:S(2)}) %copy-start) | copy-done | bytes 131096
  1.5 0.0 copy-start.1
  1.5 0.9 %copy-done.1 = bf16[14,16,256]{2,1,0:T(8,128)(2,1)S(1)} copy-done((bf16[14,16,256]{2,1,0:T(8,128)(2,1)S(1)}, bf16[14,16,256]{2,1,0:T(8,128)(2,1)}, u32[]{:S(2)}) %copy-start.1) | copy-done | bytes 114712
  2.4 0.0 copy-start.2
  2.4 0.9 %copy-done.2 = bf16[14,16,256]{2,1,0:T(8,128)(2,1)S(1)} copy-done((bf16[14,16,256]{2,1,0:T(8,128)(2,1)S(1)}, bf16[14,16,256]{2,1,0:T(8,128)(2,1)}, u32[]{:S(2)}) %copy-start.2) | copy-done | bytes 114712
  3.3 0.0 copy-start.3
  3.3 0.7 %copy-done.3 = s32[2,28]{1,0:T(2,128)S(1)} copy-done((s32[2,28]{1,0:T(2,128)S(1)}, s32[2,28]{1,0:T(2,128)}, u32[]{:S(2)}) %copy-start.3) | copy-done | bytes 248
  4.0 56.2 %shard_map.101 = (f32[14,16,256]{2,1,0:T(8,128)S(1)}, f32[256,256]{1,0:T(8,128)S(1)}, f32[14,16,256]{2,1,0:T(8,128)S(1)}, f32[256,256]{1,0:T(8,128)S(1)}, f32[256,256]{1,0:T(8,128)S(1)}) custom-call(bf16[1792,896]{1,0:T(8,128)(2,1)} %inverse_hbm.1, bf16[14,16,256]{2,1,0:T(8,128)(2,1)S(1)} %copy-done.1, bf16[14,16,256]{2,1,0:T(8,128)(2,1)S(1)} %copy-done.2, ...), custom_call_target="tpu_custom_call" | custom-call | tf_op jit(solution)/shard_map/pallas_call | solution.py:504
  60.3 0.7 %copy.16 = f32[14,16,256]{2,1,0:T(8,128)} copy(f32[14,16,256]{2,1,0:T(8,128)S(1)} %get-tuple-element.10) | data formatting | bytes 458752
  60.9 0.7 %copy.17 = f32[256,256]{1,0:T(8,128)} copy(f32[256,256]{1,0:T(8,128)S(1)} %get-tuple-element.11) | data formatting | bytes 524288
  61.6 0.7 %copy.18 = f32[14,16,256]{2,1,0:T(8,128)} copy(f32[14,16,256]{2,1,0:T(8,128)S(1)} %get-tuple-element.12) | data formatting | bytes 458752
  62.3 0.7 %copy.19 = f32[256,256]{1,0:T(8,128)} copy(f32[256,256]{1,0:T(8,128)S(1)} %get-tuple-element.13) | data formatting | bytes 524288
  63.0 0.7 %copy.20 = f32[256,256]{1,0:T(8,128)} copy(f32[256,256]{1,0:T(8,128)S(1)} %get-tuple-element.14) | data formatting | bytes 524288
Async XLA Ops:
  0.6 0.9 %copy-start = (bf16[256,256]{1,0:T(8,128)(2,1)S(1)}, bf16[256,256]{1,0:T(8,128)(2,1)}, u32[]{:S(2)}) copy-start(bf16[256,256]{1,0:T(8,128)(2,1)} %link_hbm.1) | copy-start | bytes 393220
  1.5 0.9 %copy-start.1 = (bf16[14,16,256]{2,1,0:T(8,128)(2,1)S(1)}, bf16[14,16,256]{2,1,0:T(8,128)(2,1)}, u32[]{:S(2)}) copy-start(bf16[14,16,256]{2,1,0:T(8,128)(2,1)} %late_hbm.1) | copy-start | bytes 344068
  2.4 0.9 %copy-start.2 = (bf16[14,16,256]{2,1,0:T(8,128)(2,1)S(1)}, bf16[14,16,256]{2,1,0:T(8,128)(2,1)}, u32[]{:S(2)}) copy-start(bf16[14,16,256]{2,1,0:T(8,128)(2,1)} %early_hbm.1) | copy-start | bytes 344068
  3.3 0.7 %copy-start.3 = (s32[2,28]{1,0:T(2,128)S(1)}, s32[2,28]{1,0:T(2,128)}, u32[]{:S(2)}) copy-start(s32[2,28]{1,0:T(2,128)} %structures_ref.1) | copy-start | bytes 676
